TPU v7x, 32 devices: a whole 2x2x4 slice. The times are simulated.
32 devices in a mesh: dp: 2 (over core), expert: 4 (over y, x), shard: 4 (over z).
Axes of the slice: x: 2, y: 2, z: 4, core: 2. Of those that a mesh axis runs over, the one named last changes fastest.
Arguments:
- tokens: bfloat16 [256, 4096], P('dp', 'shard'), may hold values from -6 to 6
- cotangent: bfloat16 [256, 4096], P('dp', 'shard'), may hold values from -6 to 6
- routes: int32 [256, 2], P('dp'), may hold values from 0 to 3, all different within a row; in each aligned block of 128 rows (0 to 127, 128 to 255, ...) at most 96 rows name the same one
- gate_prob: float32 [256, 2], P('dp'), may hold values from 0.2 to 1
- w_gate: bfloat16 [4, 4096, 8192], P('expert', 'shard', 'dp'), may hold values from -0.09375 to 0.09375
- w_up: bfloat16 [4, 4096, 8192], P('expert', 'shard', 'dp'), may hold values from -0.09375 to 0.09375
- w_down: bfloat16 [4, 8192, 4096], P('expert', 'dp', 'shard'), may hold values from -0.0625 to 0.0625
Outputs:
- mixed: bfloat16 [256, 4096], P('dp', 'shard')
- grad_tokens: bfloat16 [256, 4096], P('dp', 'shard')
- grad_gate: float32 [4, 4096, 8192], P('expert', 'shard', 'dp')
- grad_up: float32 [4, 4096, 8192], P('expert', 'shard', 'dp')
- grad_down: float32 [4, 8192, 4096], P('expert', 'dp', 'shard')
Inputs may be any that keep to these rules, and one draw needn't show every extreme that they name: The two routes of a row differ. In each aligned block of 128 rows no expert is named by more than 96 rows.
All inputs are finite; a program needn't handle non-finite values.
Results may differ from a plain program's by a relative error of at most 0.02.
Values may be sent and summed in bfloat16 or wider, within the bound.
A program may use at most 128 MiB of HBM per device.

v0:
```python
import jax
import jax.numpy as jnp
from jax import lax
from jax.sharding import PartitionSpec as P

CAP = 96


def silu_parts(values):
    sigma = jax.nn.sigmoid(values)
    return (values * sigma, sigma * (1.0 + values * (1.0 - sigma)))


def contract_last(left, right):
    return lax.dot_general(
        left, right, (((1,), (1,)), ((), ())), preferred_element_type=jnp.float32
    )


def contract_first(left, right):
    return lax.dot_general(
        left, right, (((0,), (0,)), ((), ())), preferred_element_type=jnp.float32
    )


def finish(gate_value, up_value, d_hidden):
    active, slope = silu_parts(gate_value)
    hidden = (active * up_value).astype(jnp.bfloat16)
    d_gate = (d_hidden * up_value * slope).astype(jnp.bfloat16)
    d_up = (d_hidden * active).astype(jnp.bfloat16)
    return (hidden, d_gate, d_up)


def per_device(tokens, cotangent, routes, gate_prob, w_gate, w_up, w_down):
    highest = lax.Precision.HIGHEST
    expert_id = lax.axis_index("expert")
    token_count = tokens.shape[0]
    positions = jnp.arange(token_count)
    below_mask = (positions[:, None] > positions[None, :]).astype(jnp.float32)
    chosen = routes == expert_id
    chosen_rows = jnp.any(chosen, axis=1).astype(jnp.float32)
    weight = jnp.sum(jnp.where(chosen, gate_prob, 0.0), axis=1)
    slot_rank = jnp.dot(below_mask, chosen_rows, precision=highest)
    slot_iota = jnp.arange(CAP).astype(jnp.float32)
    dispatch = (slot_rank[:, None] == slot_iota[None, :]).astype(jnp.float32) * chosen_rows[:, None]
    dispatch_half = dispatch.astype(jnp.bfloat16)
    x_slots = contract_first(dispatch_half, tokens).astype(jnp.bfloat16)
    dz_tok = (weight[:, None] * cotangent.astype(jnp.float32)).astype(jnp.bfloat16)
    dz_slots = contract_first(dispatch_half, dz_tok).astype(jnp.bfloat16)
    x_all, dz_all = (
        lax.all_gather(x_slots, "dp", axis=0, tiled=True),
        lax.all_gather(dz_slots, "dp", axis=0, tiled=True),
    )
    gate_w = w_gate[0]
    up_w = w_up[0]
    down_w = w_down[0]
    gate_part = jnp.dot(x_all, gate_w, preferred_element_type=jnp.float32)
    up_part = jnp.dot(x_all, up_w, preferred_element_type=jnp.float32)
    down_part = contract_last(dz_all, down_w)
    summed = (
        lax.psum_scatter(gate_part, "shard", scatter_dimension=0, tiled=True),
        lax.psum_scatter(up_part, "shard", scatter_dimension=0, tiled=True),
        lax.psum_scatter(down_part, "shard", scatter_dimension=0, tiled=True),
    )
    hidden_own, d_gate_own, d_up_own = finish(summed[0], summed[1], summed[2])
    hidden, d_gate, d_up = (
        lax.all_gather(hidden_own, "shard", axis=0, tiled=True),
        lax.all_gather(d_gate_own, "shard", axis=0, tiled=True),
        lax.all_gather(d_up_own, "shard", axis=0, tiled=True),
    )
    expert_out = jnp.dot(hidden, down_w, preferred_element_type=jnp.float32)
    slot_grad = contract_last(d_gate, gate_w) + contract_last(d_up, up_w)
    grad_down = contract_first(hidden, dz_all)
    grad_gate = contract_first(x_all, d_gate)
    grad_up = contract_first(x_all, d_up)
    out_own, grad_own = (
        lax.psum_scatter(
            expert_out.astype(jnp.bfloat16), "dp", scatter_dimension=0, tiled=True
        ).astype(jnp.float32),
        lax.psum_scatter(
            slot_grad.astype(jnp.bfloat16), "dp", scatter_dimension=0, tiled=True
        ).astype(jnp.float32),
    )
    out_tok = jnp.dot(dispatch * weight[:, None], out_own, precision=highest)
    grad_tok = jnp.dot(dispatch, grad_own, precision=highest)
    out_sum, grad_sum = (
        lax.psum(out_tok.astype(jnp.bfloat16), "expert").astype(jnp.float32),
        lax.psum(grad_tok.astype(jnp.bfloat16), "expert").astype(jnp.float32),
    )
    mixed = out_sum.astype(jnp.bfloat16)
    grad_tokens = grad_sum.astype(jnp.bfloat16)
    return (mixed, grad_tokens, grad_gate[None], grad_up[None], grad_down[None])


def solution(mesh):
    return jax.shard_map(
        per_device,
        mesh=mesh,
        in_specs=(
            P("dp", "shard"),
            P("dp", "shard"),
            P("dp", None),
            P("dp", None),
            P("expert", "shard", "dp"),
            P("expert", "shard", "dp"),
            P("expert", "dp", "shard"),
        ),
        out_specs=(
            P("dp", "shard"),
            P("dp", "shard"),
            P("expert", "shard", "dp"),
            P("expert", "shard", "dp"),
            P("expert", "dp", "shard"),
        ),
        check_vma=False,
    )
```

profile of v0, /device:TPU:0, one launch (start us, length us, event | category | flops | bytes accessed | tf_op | source)
XLA Modules:
  0.0 407.4 jit_solution(14798275414818196300)
XLA Ops:
  10.1 2.2 all_gather.17
  12.3 7.9 %fusion = f32[192,4096]{1,0:T(8,128)} fusion(bf16[192,1024]{1,0:T(8,128)(2,1)S(1)} %all_gather.17, bf16[1,4096,1024]{2,1,0:T(8,128)(2,1)} %param.13), kind=kOutput, calls=%fused_computation.3 | convolution fusion | flops 1610612736 | bytes 11927552 | tf_op jit(solution)/shard_map/dot_general | solution.py:15
  20.6 2.1 all_gather.15
  22.7 6.8 %fusion.6 = f32[192,4096]{1,0:T(8,128)} fusion(bf16[192,1024]{1,0:T(8,128)(2,1)S(1)} %all_gather.15, bf16[1,1024,4096]{2,1,0:T(8,128)(2,1)} %param.12), kind=kOutput, calls=%fused_computation.9 | convolution fusion | flops 1610612736 | bytes 11927552 | tf_op jit(solution)/shard_map/dot_general | solution.py:58
  29.7 6.9 %fusion.10 = f32[192,4096]{1,0:T(8,128)} fusion(bf16[192,1024]{1,0:T(8,128)(2,1)S(1)} %all_gather.15, bf16[1,1024,4096]{2,1,0:T(8,128)(2,1)} %param.11), kind=kOutput, calls=%fused_computation.13 | convolution fusion | flops 1610612736 | bytes 11927552 | tf_op jit(solution)/shard_map/dot_general | solution.py:57
  36.6 46.7 %reduce-scatter.12.cloned.1.call-done = f32[48,4096]{1,0:T(8,128)} async-done(((f32[192,4096]{1,0:T(8,128)}), f32[48,4096]{1,0:T(8,128)}) %reduce-scatter.12.cloned.1.call-update) | async-done | bytes 786448 | tf_op jit(solution)/shard_map/reduce_scatter | solution.py:63
  83.3 63.2 %reduce-scatter.8.cloned.1.call-done = f32[48,4096]{1,0:T(8,128)} async-done(((f32[192,4096]{1,0:T(8,128)}), f32[48,4096]{1,0:T(8,128)}) %reduce-scatter.8.cloned.1.call-update) | async-done | bytes 786448 | tf_op jit(solution)/shard_map/reduce_scatter | solution.py:62
  146.5 63.2 %reduce-scatter.6.cloned.1.call-done = f32[48,4096]{1,0:T(8,128)} async-done(((f32[192,4096]{1,0:T(8,128)}), f32[48,4096]{1,0:T(8,128)}) %reduce-scatter.6.cloned.1.call-update) | async-done | bytes 786448 | tf_op jit(solution)/shard_map/reduce_scatter | solution.py:61
  209.7 3.0 multiply_convert_fusion.1
  213.9 36.1 %all-gather.4.cloned.1.call-done = bf16[192,4096]{1,0:T(8,128)(2,1)} async-done(((bf16[48,4096]{1,0:T(8,128)(2,1)}), bf16[192,4096]{1,0:T(8,128)(2,1)}) %all-gather.4.cloned.1.call-update) | async-done | bytes 1572880 | tf_op jit(solution)/shard_map/all_gather | solution.py:67
  250.0 6.4 %fusion.15 = bf16[192,1024]{1,0:T(8,128)(2,1)} fusion(bf16[192,4096]{1,0:T(8,128)(2,1)} %all-gather.4.cloned.1.call-done, bf16[1,4096,1024]{2,1,0:T(8,128)(2,1)} %param.13), kind=kOutput, calls=%fused_computation.16 | convolution fusion | flops 1610809344 | bytes 10354688 | tf_op jit(solution)/shard_map/dot_general | solution.py:71
  256.6 31.3 %all-gather.8.cloned.1.call-done = bf16[192,4096]{1,0:T(8,128)(2,1)} async-done(((bf16[48,4096]{1,0:T(8,128)(2,1)}), bf16[192,4096]{1,0:T(8,128)(2,1)}) %all-gather.8.cloned.1.call-update) | async-done | bytes 1572880 | tf_op jit(solution)/shard_map/all_gather | solution.py:69
  287.9 6.8 %fusion.4 = f32[192,1024]{1,0:T(8,128)S(1)} fusion(bf16[192,4096]{1,0:T(8,128)(2,1)} %all-gather.8.cloned.1.call-done, bf16[1,1024,4096]{2,1,0:T(8,128)(2,1)} %param.12), kind=kOutput, calls=%fused_computation.7 | convolution fusion | flops 1610612736 | bytes 10747904 | tf_op jit(solution)/shard_map/dot_general | solution.py:15
  294.7 31.2 %all-gather.6.cloned.1.call-done = bf16[192,4096]{1,0:T(8,128)(2,1)} async-done(((bf16[48,4096]{1,0:T(8,128)(2,1)}), bf16[192,4096]{1,0:T(8,128)(2,1)}) %all-gather.6.cloned.1.call-update) | async-done | bytes 1572880 | tf_op jit(solution)/shard_map/all_gather | solution.py:68
  325.9 7.5 %fusion.18 = bf16[192,1024]{1,0:T(8,128)(2,1)} fusion(f32[192,1024]{1,0:T(8,128)S(1)} %fusion.4, bf16[192,4096]{1,0:T(8,128)(2,1)} %all-gather.6.cloned.1.call-done, bf16[1,1024,4096]{2,1,0:T(8,128)(2,1)} %param.11), kind=kOutput, calls=%fused_computation.17 | convolution fusion | flops 1611005952 | bytes 11141120 | tf_op jit(solution)/shard_map/dot_general | solution.py:15
  333.5 8.5 %convolution_bitcast_fusion = f32[1,4096,1024]{2,1,0:T(8,128)} fusion(bf16[192,4096]{1,0:T(8,128)(2,1)S(1)} %copy-done.2, bf16[192,1024]{1,0:T(8,128)(2,1)S(1)} %all_gather.17), kind=kOutput, calls=%fused_computation | convolution fusion | flops 1610612736 | bytes 18743296 | tf_op jit(solution)/shard_map/dot_general | solution.py:21
  342.1 2.0 convolution_convert_fusion.1
  344.1 3.2 reduce-scatter.14.cloned.1.call-done
  347.3 2.0 convolution_convert_fusion
  349.4 10.1 %convolution_bitcast_fusion.2 = f32[1,1024,4096]{2,1,0:T(8,128)} fusion(bf16[192,1024]{1,0:T(8,128)(2,1)S(1)} %all_gather.15, bf16[192,4096]{1,0:T(8,128)(2,1)} %all-gather.6.cloned.1.call-done), kind=kOutput, calls=%fused_computation.2 | convolution fusion | flops 1610612736 | bytes 18743296 | tf_op jit(solution)/shard_map/dot_general | solution.py:21
  359.5 8.6 %convolution_bitcast_fusion.1 = f32[1,1024,4096]{2,1,0:T(8,128)} fusion(bf16[192,1024]{1,0:T(8,128)(2,1)S(1)} %all_gather.15, bf16[192,4096]{1,0:T(8,128)(2,1)S(1)} %copy-done.3), kind=kOutput, calls=%fused_computation.1 | convolution fusion | flops 1610612736 | bytes 18743296 | tf_op jit(solution)/shard_map/dot_general | solution.py:21
  368.0 29.5 %all-reduce.3.cloned.1.call-done = (bf16[128,1024]{1,0:T(8,128)(2,1)}, bf16[128,1024]{1,0:T(8,128)(2,1)}) async-done(((bf16[128,1024]{1,0:T(8,128)(2,1)}, bf16[128,1024]{1,0:T(8,128)(2,1)}), (bf16[128,1024]{1,0:T(8,128)(2,1)}, bf16[128,1024]{1,0:T(8,128)(2,1)})) %all-reduce.3.cloned.1.call-update) | async-done | bytes 524304 | tf_op jit(solution)/shard_map/psum | solution.py:87
  397.5 1.7 copy.14
  399.2 1.7 copy.15
  (34 shorter events, 4.9 us)
Async XLA Ops:
  7.2 13.2 %copy-start = (bf16[128,1024]{1,0:T(8,128)(2,1)S(1)}, bf16[128,1024]{1,0:T(8,128)(2,1)}, u32[]{:S(2)}) copy-start(bf16[128,1024]{1,0:T(8,128)(2,1)} %param.7) | copy-start | bytes 786436
  7.2 76.1 %reduce-scatter.12.cloned.1.call-start = ((), (), s32[]{:S(2)}) async-start(), calls=%async_computation.9 | async-start | bytes 3932160 | tf_op jit(solution)/shard_map/reduce_scatter | solution.py:63
  20.3 126.2 %reduce-scatter.8.cloned.1.call-start = ((), (), s32[]{:S(2)}) async-start(), calls=%async_computation.6 | async-start | bytes 3932160 | tf_op jit(solution)/shard_map/reduce_scatter | solution.py:62
  29.6 180.1 %reduce-scatter.6.cloned.1.call-start = ((), (), s32[]{:S(2)}) async-start(), calls=%async_computation.5 | async-start | bytes 3932160 | tf_op jit(solution)/shard_map/reduce_scatter | solution.py:61
  36.5 213.4 %all-gather.4.cloned.1.call-start = ((), (), s32[]{:S(2)}) async-start(), calls=%async_computation.7 | async-start | bytes 1966080 | tf_op jit(solution)/shard_map/all_gather | solution.py:67
  212.7 75.3 %all-gather.8.cloned.1.call-start = ((), (), s32[]{:S(2)}) async-start(), calls=%async_computation.11 | async-start | bytes 1966080 | tf_op jit(solution)/shard_map/all_gather | solution.py:69
  213.3 112.7 %all-gather.6.cloned.1.call-start = ((), (), s32[]{:S(2)}) async-start(), calls=%async_computation.10 | async-start | bytes 1966080 | tf_op jit(solution)/shard_map/all_gather | solution.py:68
  213.8 128.2 %reduce-scatter.10.cloned.1.call-start = ((), (), s32[]{:S(2)}) async-start(), calls=%async_computation.8 | async-start | bytes 589824 | tf_op jit(solution)/shard_map/reduce_scatter | solution.py:77
  256.4 90.9 %reduce-scatter.14.cloned.1.call-start = ((), (), s32[]{:S(2)}) async-start(), calls=%async_computation.12 | async-start | bytes 589824 | tf_op jit(solution)/shard_map/reduce_scatter | solution.py:80
  294.7 38.8 %copy-start.2 = (bf16[192,4096]{1,0:T(8,128)(2,1)S(1)}, bf16[192,4096]{1,0:T(8,128)(2,1)}, u32[]{:S(2)}) copy-start(bf16[192,4096]{1,0:T(8,128)(2,1)} %all-gather.4.cloned.1.call-done) | copy-start | bytes 4718596
  333.5 64.1 %all-reduce.3.cloned.1.call-start = ((), (), s32[]{:S(2)}) async-start(), calls=%async_computation.13 | async-start | bytes 1048576 | tf_op jit(solution)/shard_map/psum | solution.py:87
  349.4 10.1 %copy-start.3 = (bf16[192,4096]{1,0:T(8,128)(2,1)S(1)}, bf16[192,4096]{1,0:T(8,128)(2,1)}, u32[]{:S(2)}) copy-start(bf16[192,4096]{1,0:T(8,128)(2,1)} %all-gather.8.cloned.1.call-done) | copy-start | bytes 4718596
  349.4 51.5 %copy-start.1 = (bf16[128,1024]{1,0:T(8,128)(2,1)S(1)}, bf16[128,1024]{1,0:T(8,128)(2,1)}, u32[]{:S(2)}) copy-start(bf16[128,1024]{1,0:T(8,128)(2,1)} %param.7) | copy-start | bytes 786436
Sparse Core Ops, SparseCore 0:
  20.4 62.8 reduce-scatter.11
  86.2 60.2 reduce-scatter.7
  149.3 60.2 reduce-scatter.5
  212.8 37.1 all-gather.3
  251.9 35.9 all-gather.7
  289.9 35.9 all-gather.5
  328.7 6.6 reduce-scatter.9
  338.3 8.9 reduce-scatter.13
  350.8 46.6 all-reduce.2
where the time goes:
time: 408 us; the launch traced here: 407 us
  waiting for transfers between devices  305 us (75%)
  matrix products  75.3 us (18%)
  between operations  13.9 us (3%)
  other arithmetic  4.45 us (1%)
  blocking collectives  4.27 us (1%)
    reduce_scatter x1, waiting for transfers between devices, per_device(): lax.psum_scatter(gate_part, 'shard', scatter_dimension=0, tiled=True)  63.2 us
    reduce_scatter x1, waiting for transfers between devices, per_device(): lax.psum_scatter(up_part, 'shard', scatter_dimension=0, tiled=True)  63.2 us
    reduce_scatter x1, waiting for transfers between devices, per_device(): lax.psum_scatter(down_part, 'shard', scatter_dimension=0, tiled=True)  46.7 us
    all_gather x1, waiting for transfers between devices, per_device(): lax.all_gather(hidden_own, 'shard', axis=0, tiled=True)  36.1 us
    all_gather x1, waiting for transfers between devices, per_device(): lax.all_gather(d_up_own, 'shard', axis=0, tiled=True)  31.3 us
    all_gather x1, waiting for transfers between devices, per_device(): lax.all_gather(d_gate_own, 'shard', axis=0, tiled=True)  31.2 us
    psum x1, waiting for transfers between devices, per_device(): lax.psum(out_tok.astype(jnp.bfloat16), 'expert').astype(jnp.float32)  29.5 us
    dot_general x5, matrix products, contract_first(): lax.dot_general(left, right, (((0,), (0,)), ((), ())), preferred_element_...  28.8 us
  transfers between devices with their start and end apart: 9, of which 8 were waited for; matrix products, arithmetic and copies ran while one was open for 16% of the time, Pallas kernels for 0%

commit v1 on v0

v1 whole, which is shorter than its diff:
```python
import functools

import jax
import jax.numpy as jnp
from jax import lax
from jax.experimental import pallas as pl
from jax.experimental.pallas import tpu as pltpu
from jax.sharding import PartitionSpec as P

CAP = 96
WIDTH = 128
AHEAD = 2
MESH = pl.DeviceIdType.MESH
F32 = jnp.float32
BF16 = jnp.bfloat16


def dot_nn(left, right):
    return lax.dot_general(left, right, (((1,), (0,)), ((), ())), preferred_element_type=F32)


def dot_nt(left, right):
    return lax.dot_general(left, right, (((1,), (1,)), ((), ())), preferred_element_type=F32)


def dot_tn(left, right):
    return lax.dot_general(left, right, (((0,), (0,)), ((), ())), preferred_element_type=F32)


def exchange_kernel(
    n, n_dp, chunks,
    tok, cot, routes, prob, wg, wu, wd,
    tok_out, act_out, x_out, dz_out,
    wgv, wuv, wdv, part, from_left, from_right, to_right, to_left,
    x_v, dz_v, acc_o, acc_g, stage, landed, disp, wgt,
    w_sem, sr_sem, rr_sem, sl_sem, rl_sem, act_sem, xo_sem,
    xs_sem, xr_sem, os_sem, or_sem,
):
    f = WIDTH
    s = lax.axis_index("shard")
    d = lax.axis_index("dp")
    e = lax.axis_index("expert")
    act = from_left
    n_part = part.shape[0]
    n_stage = to_right.shape[0]
    t = tok.shape[0]

    def w_copies(c):
        cols = pl.ds(pl.multiple_of(c * f, f), f)
        return (
            pltpu.make_async_copy(wg.at[:, cols], wgv.at[c], w_sem.at[0, c]),
            pltpu.make_async_copy(wu.at[:, cols], wuv.at[c], w_sem.at[1, c]),
            pltpu.make_async_copy(wd.at[cols, :], wdv.at[c], w_sem.at[2, c]),
        )

    @pl.loop(0, chunks)
    def _(c):
        for copy in w_copies(c):
            copy.start()

    barrier = pltpu.get_barrier_semaphore()

    @pl.when(s > 0)
    def _():
        pl.semaphore_signal(barrier, inc=1, device_id={"shard": s - 1}, device_id_type=MESH)

    @pl.when(s < n - 1)
    def _():
        pl.semaphore_signal(barrier, inc=1, device_id={"shard": s + 1}, device_id_type=MESH)

    for k in range(1, n_dp):
        pl.semaphore_signal(
            barrier, inc=1, device_id={"dp": lax.rem(d + k, n_dp)}, device_id_type=MESH
        )

    chosen = routes[...] == e
    picked = jnp.max(chosen.astype(F32), axis=1, keepdims=True)
    weight = jnp.sum(jnp.where(chosen, prob[...], 0.0), axis=1, keepdims=True)
    rows_i = lax.broadcasted_iota(jnp.int32, (t, t), 0)
    cols_i = lax.broadcasted_iota(jnp.int32, (t, t), 1)
    below = (rows_i > cols_i).astype(F32).astype(BF16)
    rank = dot_nn(below, jnp.broadcast_to(picked, (t, t)).astype(BF16))[:, :CAP]
    slot = lax.broadcasted_iota(jnp.int32, (t, CAP), 1).astype(F32)
    dispatch = jnp.where(rank == slot, jnp.broadcast_to(picked, (t, CAP)), 0.0).astype(BF16)
    disp[...] = dispatch
    wgt[...] = jnp.broadcast_to(weight, wgt.shape)
    mine = pl.ds(pl.multiple_of(d * CAP, CAP), CAP)
    x_v[mine, :] = dot_tn(dispatch, tok[...]).astype(BF16)
    dz_tok = (weight * cot[...].astype(F32)).astype(BF16)
    dz_v[mine, :] = dot_tn(dispatch, dz_tok).astype(BF16)

    pl.semaphore_wait(barrier, (s > 0).astype(jnp.int32) + (s < n - 1).astype(jnp.int32) + (n_dp - 1))

    def slot_copy(ref, k, row, sem_row, to):
        rows = pl.ds(pl.multiple_of(row * CAP, CAP), CAP)
        return pltpu.make_async_remote_copy(
            src_ref=ref.at[rows], dst_ref=ref.at[rows],
            send_sem=xs_sem.at[k, to], recv_sem=xr_sem.at[k, sem_row],
            device_id={"dp": to}, device_id_type=MESH,
        )

    for j in range(1, n_dp):
        to = lax.rem(d + j, n_dp)
        slot_copy(x_v, 0, d, d, to).start()
        slot_copy(dz_v, 1, d, d, to).start()
    acc_o[...] = jnp.zeros_like(acc_o)
    acc_g[...] = jnp.zeros_like(acc_g)
    for j in range(1, n_dp):
        other = lax.rem(d + j, n_dp)
        slot_copy(x_v, 0, other, other, other).wait_recv()
        slot_copy(dz_v, 1, other, other, other).wait_recv()
    for j in range(1, n_dp):
        to = lax.rem(d + j, n_dp)
        slot_copy(x_v, 0, d, d, to).wait_send()
        slot_copy(dz_v, 1, d, d, to).wait_send()
    x_store = pltpu.make_async_copy(x_v, x_out, xo_sem.at[0])
    dz_store = pltpu.make_async_copy(dz_v, dz_out, xo_sem.at[1])
    x_store.start()
    dz_store.start()

    def right_copy(c):
        here = lax.rem(c, n_stage)
        return pltpu.make_async_remote_copy(
            src_ref=to_right.at[here], dst_ref=from_left.at[c],
            send_sem=sr_sem.at[here], recv_sem=rr_sem.at[c],
            device_id={"shard": lax.min(s + 1, n - 1)}, device_id_type=MESH,
        )

    def left_copy(c):
        here = lax.rem(c, n_stage)
        return pltpu.make_async_remote_copy(
            src_ref=to_left.at[here], dst_ref=from_right.at[c],
            send_sem=sl_sem.at[here], recv_sem=rl_sem.at[c],
            device_id={"shard": lax.max(s - 1, 0)}, device_id_type=MESH,
        )

    def send(copy_of, buffer, c, value):
        @pl.when(c >= n_stage)
        def _():
            copy_of(c - n_stage).wait_send()

        buffer[lax.rem(c, n_stage)] = value().astype(BF16)
        copy_of(c).start()

    @pl.loop(0, chunks + AHEAD + n - 1)
    def _(i):
        @pl.when(i < chunks)
        def _():
            for copy in w_copies(i):
                copy.wait()
            p = lax.rem(i, n_part)
            part[p, :, 0:f] = dot_nn(x_v[...], wgv[i])
            part[p, :, f:2 * f] = dot_nn(x_v[...], wuv[i])
            part[p, :, 2 * f:3 * f] = dot_nt(dz_v[...], wdv[i])

            @pl.when((s == 0) & (n > 1))
            def _():
                send(right_copy, to_right, i, lambda: part[p])

            @pl.when((s == n - 1) & (n > 1))
            def _():
                send(left_copy, to_left, i, lambda: part[p])

        r = i - AHEAD - s

        @pl.when((s > 0) & (r >= 0) & (r < chunks))
        def _():
            right_copy(r).wait_recv()

            @pl.when(s < n - 1)
            def _():
                send(right_copy, to_right, r, lambda: part[lax.rem(r, n_part)] + from_left[r].astype(F32))

        q = i - AHEAD - (n - 1 - s)

        @pl.when((s < n - 1) & (q >= 0) & (q < chunks))
        def _():
            left_copy(q).wait_recv()

            @pl.when(s > 0)
            def _():
                send(left_copy, to_left, q, lambda: part[lax.rem(q, n_part)] + from_right[q].astype(F32))

        c = i - AHEAD - lax.max(s, n - 1 - s)

        @pl.when((c >= 0) & (c < chunks))
        def _():
            p = lax.rem(c, n_part)

            @pl.when(s > 0)
            def _():
                part[p] += from_left[c].astype(F32)

            @pl.when(s < n - 1)
            def _():
                part[p] += from_right[c].astype(F32)

            gate = part[p, :, 0:f]
            up = part[p, :, f:2 * f]
            d_hidden = part[p, :, 2 * f:3 * f]
            sigma = jax.nn.sigmoid(gate)
            active = gate * sigma
            slope = sigma * (1.0 + gate * (1.0 - sigma))
            hidden = (active * up).astype(BF16)
            d_gate = (d_hidden * up * slope).astype(BF16)
            d_up = (d_hidden * active).astype(BF16)
            act[c, :, 0:f] = hidden
            act[c, :, f:2 * f] = d_gate
            act[c, :, 2 * f:3 * f] = d_up
            pltpu.make_async_copy(act.at[c], act_out.at[c], act_sem.at[c]).start()
            acc_o[...] += dot_nn(hidden, wdv[c])
            acc_g[...] += dot_nt(d_gate, wgv[c]) + dot_nt(d_up, wuv[c])

    stage[0] = acc_o[...].astype(BF16)
    stage[1] = acc_g[...].astype(BF16)

    def sum_copy(k, to, sender):
        return pltpu.make_async_remote_copy(
            src_ref=stage.at[k, pl.ds(pl.multiple_of(to * CAP, CAP), CAP)],
            dst_ref=landed.at[k, pl.ds(pl.multiple_of(sender * CAP, CAP), CAP)],
            send_sem=os_sem.at[k, to], recv_sem=or_sem.at[k, sender],
            device_id={"dp": to}, device_id_type=MESH,
        )

    for k in range(2):
        for j in range(1, n_dp):
            sum_copy(k, lax.rem(d + j, n_dp), d).start()
    for k in range(2):
        own = (acc_o, acc_g)[k][mine, :]
        for j in range(1, n_dp):
            other = lax.rem(d + j, n_dp)
            sum_copy(k, other, other).wait_recv()
            own = own + landed[k, pl.ds(pl.multiple_of(other * CAP, CAP), CAP), :].astype(F32)
        rows = dot_nn(disp[...], own.astype(BF16))
        if k == 0:
            rows = rows * wgt[:, 0:1]
        tok_out[k] = rows.astype(BF16)

    for k in range(2):
        for j in range(1, n_dp):
            sum_copy(k, lax.rem(d + j, n_dp), d).wait_send()
    x_store.wait()
    dz_store.wait()

    @pl.loop(0, chunks)
    def _(c):
        pltpu.make_async_copy(act.at[c], act_out.at[c], act_sem.at[c]).wait()

    @pl.loop(max(chunks - n_stage, 0), chunks)
    def _(c):
        @pl.when(s < n - 1)
        def _():
            right_copy(c).wait_send()

        @pl.when(s > 0)
        def _():
            left_copy(c).wait_send()


def grads_kernel(act, x, dz, gate_out, up_out, down_out, x_t):
    f = WIDTH

    @pl.when(pl.program_id(0) == 0)
    def _():
        x_t[...] = x[...].T

    for c in range(act.shape[0]):
        cols = slice(c * f, (c + 1) * f)
        gate_out[:, cols] = dot_nn(x_t[...], act[c, :, f:2 * f])
        up_out[:, cols] = dot_nn(x_t[...], act[c, :, 2 * f:3 * f])
        down_out[cols, :] = dot_tn(act[c, :, 0:f], dz[...])


def per_device(n, n_dp, tokens, cotangent, routes, gate_prob, w_gate, w_up, w_down):
    t, dl = tokens.shape
    ffl = w_gate.shape[2]
    f = WIDTH
    chunks = ffl // f
    rows = n_dp * CAP
    n_part = min(n + AHEAD, chunks)
    n_stage = max(1, min(4, chunks // 2))
    vmem = pl.BlockSpec(memory_space=pltpu.VMEM)
    hbm = pl.BlockSpec(memory_space=pl.ANY)
    tok_part, act, x_all, dz_all = pl.pallas_call(
        functools.partial(exchange_kernel, n, n_dp, chunks),
        out_shape=(
            jax.ShapeDtypeStruct((2, t, dl), BF16),
            jax.ShapeDtypeStruct((chunks, rows, 3 * f), BF16),
            jax.ShapeDtypeStruct((rows, dl), BF16),
            jax.ShapeDtypeStruct((rows, dl), BF16),
        ),
        in_specs=[vmem] * 4 + [hbm] * 3,
        out_specs=(vmem, hbm, hbm, hbm),
        scratch_shapes=[
            pltpu.VMEM((chunks, dl, f), BF16),
            pltpu.VMEM((chunks, dl, f), BF16),
            pltpu.VMEM((chunks, f, dl), BF16),
            pltpu.VMEM((n_part, rows, 3 * f), F32),
            pltpu.VMEM((chunks, rows, 3 * f), BF16),
            pltpu.VMEM((chunks, rows, 3 * f), BF16),
            pltpu.VMEM((n_stage, rows, 3 * f), BF16),
            pltpu.VMEM((n_stage, rows, 3 * f), BF16),
            pltpu.VMEM((rows, dl), BF16),
            pltpu.VMEM((rows, dl), BF16),
            pltpu.VMEM((rows, dl), F32),
            pltpu.VMEM((rows, dl), F32),
            pltpu.VMEM((2, rows, dl), BF16),
            pltpu.VMEM((2, rows, dl), BF16),
            pltpu.VMEM((t, CAP), BF16),
            pltpu.VMEM((t, 128), F32),
            pltpu.SemaphoreType.DMA((3, chunks)),
            pltpu.SemaphoreType.DMA((n_stage,)),
            pltpu.SemaphoreType.DMA((chunks,)),
            pltpu.SemaphoreType.DMA((n_stage,)),
            pltpu.SemaphoreType.DMA((chunks,)),
            pltpu.SemaphoreType.DMA((chunks,)),
            pltpu.SemaphoreType.DMA((2,)),
            pltpu.SemaphoreType.DMA((2, n_dp)),
            pltpu.SemaphoreType.DMA((2, n_dp)),
            pltpu.SemaphoreType.DMA((2, n_dp)),
            pltpu.SemaphoreType.DMA((2, n_dp)),
        ],
        compiler_params=pltpu.CompilerParams(
            collective_id=0, has_side_effects=True, vmem_limit_bytes=63 * 1024 * 1024
        ),
        cost_estimate=pl.CostEstimate(
            flops=12 * rows * dl * ffl, bytes_accessed=6 * dl * ffl, transcendentals=rows * ffl
        ),
    )(tokens, cotangent, routes, gate_prob, w_gate[0], w_up[0], w_down[0])
    total = lax.psum(tok_part, "expert")
    group = next(g for g in (4, 2, 1) if chunks % g == 0)
    grad_gate, grad_up, grad_down = pl.pallas_call(
        grads_kernel,
        grid=(chunks // group,),
        out_shape=(
            jax.ShapeDtypeStruct((dl, ffl), F32),
            jax.ShapeDtypeStruct((dl, ffl), F32),
            jax.ShapeDtypeStruct((ffl, dl), F32),
        ),
        in_specs=[
            pl.BlockSpec((group, rows, 3 * f), lambda j: (j, 0, 0)),
            pl.BlockSpec((rows, dl), lambda j: (0, 0)),
            pl.BlockSpec((rows, dl), lambda j: (0, 0)),
        ],
        out_specs=(
            pl.BlockSpec((dl, group * f), lambda j: (0, j)),
            pl.BlockSpec((dl, group * f), lambda j: (0, j)),
            pl.BlockSpec((group * f, dl), lambda j: (j, 0)),
        ),
        scratch_shapes=[pltpu.VMEM((dl, rows), BF16)],
        compiler_params=pltpu.CompilerParams(vmem_limit_bytes=48 * 1024 * 1024),
        cost_estimate=pl.CostEstimate(
            flops=6 * rows * dl * ffl, bytes_accessed=12 * dl * ffl, transcendentals=0
        ),
    )(act, x_all, dz_all)
    return (total[0], total[1], grad_gate[None], grad_up[None], grad_down[None])


def solution(mesh):
    return jax.shard_map(
        functools.partial(per_device, mesh.shape["shard"], mesh.shape["dp"]),
        mesh=mesh,
        in_specs=(
            P("dp", "shard"),
            P("dp", "shard"),
            P("dp", None),
            P("dp", None),
            P("expert", "shard", "dp"),
            P("expert", "shard", "dp"),
            P("expert", "dp", "shard"),
        ),
        out_specs=(
            P("dp", "shard"),
            P("dp", "shard"),
            P("expert", "shard", "dp"),
            P("expert", "shard", "dp"),
            P("expert", "dp", "shard"),
        ),
        check_vma=False,
    )
```

time: 408 us -> 201 us (0.49)
  waiting for transfers between devices: 305 us -> 21.3 us
  Pallas kernels: 0 us -> 157 us
  matrix products: 75.3 us -> 0 us
  local copies, waits for them, and re-layouts: 3.36 us -> 9.02 us
  other arithmetic: 4.45 us -> 0 us
  blocking collectives: 4.27 us -> 0 us
    reduce_scatter x5 -> x0, waiting for transfers between devices: 176 us -> none  [the longest x1 63.2 us: per_device(): lax.psum_scatter(gate_part, 'shard', scatter_dimension=0, tiled=True)]
    pallas_call x0 -> x2, Pallas kernels: none -> 157 us  [the longest x1 138 us: per_device(): pl.pallas_call(functools.partial(exchange_kernel, n, n_dp, chunks), out_s...]
    all_gather x3 -> x0, waiting for transfers between devices: 98.6 us -> none  [the longest x1 36.1 us: per_device(): lax.all_gather(hidden_own, 'shard', axis=0, tiled=True)]
    dot_general x14 -> x0, matrix products: 75.3 us -> none  [the longest x5 28.8 us: contract_first(): lax.dot_general(left, right, (((0,), (0,)), ((), ())), preferred_element_...]
    psum x1, waiting for transfers between devices: 29.5 us -> 21.3 us  [per_device(): total = lax.psum(tok_part, 'expert')]
    all_gather x2 -> x0, blocking collectives: 4.27 us -> none  [the longest x1 2.17 us: per_device(): lax.all_gather(dz_slots, 'dp', axis=0, tiled=True)]
  transfers between devices with their start and end apart: 9 -> 1, of which waited for: 8 -> 1; matrix products, arithmetic and copies ran while one was open for 16% -> 0% of each run, Pallas kernels for 0% -> 9%
where the time goes in v1:
time: 201 us
  Pallas kernels  157 us (78%)
  waiting for transfers between devices  21.3 us (11%)
  between operations  14 us (7%)
  local copies, waits for them, and re-layouts  9.02 us (4%)
    pallas_call x1, Pallas kernels, per_device(): pl.pallas_call(functools.partial(exchange_kernel, n, n_dp, chunks), out_s...  138 us
    psum x1, waiting for transfers between devices, per_device(): total = lax.psum(tok_part, 'expert')  21.3 us
    pallas_call x1, Pallas kernels, per_device(): pl.pallas_call(grads_kernel, grid=(chunks // group,), out_shape=(jax.Shap...  18.3 us
    unnamed x8, local copies, waits for them, and re-layouts  7.17 us
  transfers between devices with their start and end apart: 1, of which 1 were waited for; matrix products, arithmetic and copies ran while one was open for 0% of the time, Pallas kernels for 9%

profile of v1, /device:TPU:0, one launch (start us, length us, event | category | flops | bytes accessed | tf_op | source)
XLA Modules:
  0.0 201.1 jit_solution(6137378900945238936)
XLA Ops:
  7.2 0.0 all-reduce.2.cloned.1.call-start
  7.2 1.4 copy.12.routes
  8.6 1.4 copy.13.prob
  10.0 138.4 %shard_map.110 = (bf16[2,128,1024]{2,1,0:T(8,128)(2,1)}, bf16[32,192,384]{2,1,0:T(8,128)(2,1)}, bf16[192,1024]{1,0:T(8,128)(2,1)}, bf16[192,1024]{1,0:T(8,128)(2,1)}) custom-call(bf16[128,1024]{1,0:T(8,128)(2,1)} %tok.1, bf16[128,1024]{1,0:T(8,128)(2,1)} %cot.1, s32[128,2]{1,0:T(8,128)} %copy.12.routes, f32[128,2]{1,0:T(8,128)} %copy.13.prob, ...), custom_call_target="tpu_custom_call" | custom-call | flops 9663676416 | bytes 25165824 | tf_op jit(solution)/shard_map/pallas_call | solution.py:284
  148.5 0.0 all-reduce.2.cloned.1.call-update
  148.5 0.0 copy-start
  148.5 2.3 %copy-done = bf16[32,192,384]{2,1,0:T(8,128)(2,1)S(1)} copy-done((bf16[32,192,384]{2,1,0:T(8,128)(2,1)S(1)}, bf16[32,192,384]{2,1,0:T(8,128)(2,1)}, u32[]{:S(2)}) %copy-start) | copy-done | bytes 4718616
  150.9 0.0 copy-start.1
  150.9 1.0 copy-done.1
  151.8 0.0 copy-start.2
  151.8 1.0 copy-done.2
  152.9 18.3 %shard_map.111 = (f32[1024,4096]{1,0:T(8,128)}, f32[1024,4096]{1,0:T(8,128)}, f32[4096,1024]{1,0:T(8,128)}) custom-call(bf16[32,192,384]{2,1,0:T(8,128)(2,1)S(1)} %copy-done, bf16[192,1024]{1,0:T(8,128)(2,1)S(1)} %copy-done.1, bf16[192,1024]{1,0:T(8,128)(2,1)S(1)} %copy-done.2), custom_call_target="tpu_custom_call" | custom-call | flops 4831838208 | bytes 50331648 | tf_op jit(solution)/shard_map/pallas_call | solution.py:332
  171.2 21.3 %all-reduce.2.cloned.1.call-done = bf16[2,128,1024]{2,1,0:T(8,128)(2,1)} async-done(((bf16[2,128,1024]{2,1,0:T(8,128)(2,1)}), bf16[2,128,1024]{2,1,0:T(8,128)(2,1)}) %all-reduce.2.cloned.1.call-update) | async-done | bytes 524304 | tf_op jit(solution)/shard_map/psum | solution.py:330
  192.4 1.9 slice_bitcast_fusion
Async XLA Ops:
  7.2 185.3 %all-reduce.2.cloned.1.call-start = ((), (), s32[]{:S(2)}) async-start(), calls=%async_computation | async-start | bytes 1048576 | tf_op jit(solution)/shard_map/psum | solution.py:330
  148.5 2.3 %copy-start = (bf16[32,192,384]{2,1,0:T(8,128)(2,1)S(1)}, bf16[32,192,384]{2,1,0:T(8,128)(2,1)}, u32[]{:S(2)}) copy-start(bf16[32,192,384]{2,1,0:T(8,128)(2,1)} %get-tuple-element.13.act) | copy-start | bytes 14155780
  150.9 1.0 copy-start.1
  151.8 1.0 copy-start.2
Sparse Core Ops, SparseCore 0:
  148.6 43.7 all-reduce.1

commit v2 on v1

--- a/solution.py
+++ b/solution.py
@@ -9,7 +9,8 @@
 
 CAP = 96
 WIDTH = 128
-AHEAD = 2
+HOP = 3
+EARLY = 8
 MESH = pl.DeviceIdType.MESH
 F32 = jnp.float32
 BF16 = jnp.bfloat16
@@ -30,7 +31,7 @@
 def exchange_kernel(
     n, n_dp, chunks,
     tok, cot, routes, prob, wg, wu, wd,
-    tok_out, act_out, x_out, dz_out,
+    mix_out, grad_out, act_out, x_out, dz_out,
     wgv, wuv, wdv, part, from_left, from_right, to_right, to_left,
     x_v, dz_v, acc_o, acc_g, stage, landed, disp, wgt,
     w_sem, sr_sem, rr_sem, sl_sem, rl_sem, act_sem, xo_sem,
@@ -53,7 +54,7 @@
             pltpu.make_async_copy(wd.at[cols, :], wdv.at[c], w_sem.at[2, c]),
         )
 
-    @pl.loop(0, chunks)
+    @pl.loop(0, min(EARLY, chunks))
     def _(c):
         for copy in w_copies(c):
             copy.start()
@@ -74,20 +75,21 @@
         )
 
     chosen = routes[...] == e
-    picked = jnp.max(chosen.astype(F32), axis=1, keepdims=True)
-    weight = jnp.sum(jnp.where(chosen, prob[...], 0.0), axis=1, keepdims=True)
+    picked = jnp.max(chosen.astype(F32), axis=0, keepdims=True)
+    weight_row = jnp.sum(jnp.where(chosen, prob[...], 0.0), axis=0, keepdims=True)
+    weight = jnp.broadcast_to(weight_row, (t, t)).T[:, 0:1]
     rows_i = lax.broadcasted_iota(jnp.int32, (t, t), 0)
     cols_i = lax.broadcasted_iota(jnp.int32, (t, t), 1)
-    below = (rows_i > cols_i).astype(F32).astype(BF16)
-    rank = dot_nn(below, jnp.broadcast_to(picked, (t, t)).astype(BF16))[:, :CAP]
-    slot = lax.broadcasted_iota(jnp.int32, (t, CAP), 1).astype(F32)
-    dispatch = jnp.where(rank == slot, jnp.broadcast_to(picked, (t, CAP)), 0.0).astype(BF16)
+    above = (rows_i < cols_i).astype(F32).astype(BF16)
+    rank = dot_nn(jnp.broadcast_to(picked, (CAP, t)).astype(BF16), above)
+    slot = lax.broadcasted_iota(jnp.int32, (CAP, t), 0).astype(F32)
+    dispatch = jnp.where(rank == slot, jnp.broadcast_to(picked, (CAP, t)), 0.0).astype(BF16)
     disp[...] = dispatch
     wgt[...] = jnp.broadcast_to(weight, wgt.shape)
     mine = pl.ds(pl.multiple_of(d * CAP, CAP), CAP)
-    x_v[mine, :] = dot_tn(dispatch, tok[...]).astype(BF16)
+    x_v[mine, :] = dot_nn(dispatch, tok[...]).astype(BF16)
     dz_tok = (weight * cot[...].astype(F32)).astype(BF16)
-    dz_v[mine, :] = dot_tn(dispatch, dz_tok).astype(BF16)
+    dz_v[mine, :] = dot_nn(dispatch, dz_tok).astype(BF16)
 
     pl.semaphore_wait(barrier, (s > 0).astype(jnp.int32) + (s < n - 1).astype(jnp.int32) + (n_dp - 1))
 
@@ -142,12 +144,18 @@
         buffer[lax.rem(c, n_stage)] = value().astype(BF16)
         copy_of(c).start()
 
-    @pl.loop(0, chunks + AHEAD + n - 1)
+    @pl.loop(0, chunks + HOP * (n - 1))
     def _(i):
         @pl.when(i < chunks)
         def _():
             for copy in w_copies(i):
                 copy.wait()
+
+            @pl.when(i + EARLY < chunks)
+            def _():
+                for copy in w_copies(i + EARLY):
+                    copy.start()
+
             p = lax.rem(i, n_part)
             part[p, :, 0:f] = dot_nn(x_v[...], wgv[i])
             part[p, :, f:2 * f] = dot_nn(x_v[...], wuv[i])
@@ -161,7 +169,7 @@
             def _():
                 send(left_copy, to_left, i, lambda: part[p])
 
-        r = i - AHEAD - s
+        r = i - HOP * s
 
         @pl.when((s > 0) & (r >= 0) & (r < chunks))
         def _():
@@ -171,7 +179,7 @@
             def _():
                 send(right_copy, to_right, r, lambda: part[lax.rem(r, n_part)] + from_left[r].astype(F32))
 
-        q = i - AHEAD - (n - 1 - s)
+        q = i - HOP * (n - 1 - s)
 
         @pl.when((s < n - 1) & (q >= 0) & (q < chunks))
         def _():
@@ -181,7 +189,7 @@
             def _():
                 send(left_copy, to_left, q, lambda: part[lax.rem(q, n_part)] + from_right[q].astype(F32))
 
-        c = i - AHEAD - lax.max(s, n - 1 - s)
+        c = i - HOP * lax.max(s, n - 1 - s)
 
         @pl.when((c >= 0) & (c < chunks))
         def _():
@@ -231,10 +239,10 @@
             other = lax.rem(d + j, n_dp)
             sum_copy(k, other, other).wait_recv()
             own = own + landed[k, pl.ds(pl.multiple_of(other * CAP, CAP), CAP), :].astype(F32)
-        rows = dot_nn(disp[...], own.astype(BF16))
+        rows = dot_tn(disp[...], own.astype(BF16))
         if k == 0:
             rows = rows * wgt[:, 0:1]
-        tok_out[k] = rows.astype(BF16)
+        (mix_out, grad_out)[k][...] = rows.astype(BF16)
 
     for k in range(2):
         for j in range(1, n_dp):
@@ -257,7 +265,7 @@
             left_copy(c).wait_send()
 
 
-def grads_kernel(act, x, dz, gate_out, up_out, down_out, x_t):
+def grads_in_kernel(act, x, gate_out, up_out, x_t):
     f = WIDTH
 
     @pl.when(pl.program_id(0) == 0)
@@ -268,29 +276,42 @@
         cols = slice(c * f, (c + 1) * f)
         gate_out[:, cols] = dot_nn(x_t[...], act[c, :, f:2 * f])
         up_out[:, cols] = dot_nn(x_t[...], act[c, :, 2 * f:3 * f])
-        down_out[cols, :] = dot_tn(act[c, :, 0:f], dz[...])
-
-
-def per_device(n, n_dp, tokens, cotangent, routes, gate_prob, w_gate, w_up, w_down):
+
+
+def grad_down_kernel(act, dz, down_out):
+    f = WIDTH
+    for c in range(act.shape[0]):
+        down_out[c * f:(c + 1) * f, :] = dot_tn(act[c, :, 0:f], dz[...])
+
+
+def expert_sum(value, n_expert, bits):
+    for bit in bits:
+        other = lax.ppermute(value, "expert", [(i, i ^ bit) for i in range(n_expert)])
+        value = (value.astype(F32) + other.astype(F32)).astype(BF16)
+    return value
+
+
+def per_device(n, n_dp, n_expert, tokens, cotangent, routes, gate_prob, w_gate, w_up, w_down):
     t, dl = tokens.shape
     ffl = w_gate.shape[2]
     f = WIDTH
     chunks = ffl // f
     rows = n_dp * CAP
-    n_part = min(n + AHEAD, chunks)
+    n_part = min(HOP * (n - 1) + 1, chunks)
     n_stage = max(1, min(4, chunks // 2))
     vmem = pl.BlockSpec(memory_space=pltpu.VMEM)
     hbm = pl.BlockSpec(memory_space=pl.ANY)
-    tok_part, act, x_all, dz_all = pl.pallas_call(
+    mix_part, grad_part, act, x_all, dz_all = pl.pallas_call(
         functools.partial(exchange_kernel, n, n_dp, chunks),
         out_shape=(
-            jax.ShapeDtypeStruct((2, t, dl), BF16),
+            jax.ShapeDtypeStruct((t, dl), BF16),
+            jax.ShapeDtypeStruct((t, dl), BF16),
             jax.ShapeDtypeStruct((chunks, rows, 3 * f), BF16),
             jax.ShapeDtypeStruct((rows, dl), BF16),
             jax.ShapeDtypeStruct((rows, dl), BF16),
         ),
         in_specs=[vmem] * 4 + [hbm] * 3,
-        out_specs=(vmem, hbm, hbm, hbm),
+        out_specs=(vmem, vmem, hbm, hbm, hbm),
         scratch_shapes=[
             pltpu.VMEM((chunks, dl, f), BF16),
             pltpu.VMEM((chunks, dl, f), BF16),
@@ -306,7 +327,7 @@
             pltpu.VMEM((rows, dl), F32),
             pltpu.VMEM((2, rows, dl), BF16),
             pltpu.VMEM((2, rows, dl), BF16),
-            pltpu.VMEM((t, CAP), BF16),
+            pltpu.VMEM((CAP, t), BF16),
             pltpu.VMEM((t, 128), F32),
             pltpu.SemaphoreType.DMA((3, chunks)),
             pltpu.SemaphoreType.DMA((n_stage,)),
@@ -326,39 +347,44 @@
         cost_estimate=pl.CostEstimate(
             flops=12 * rows * dl * ffl, bytes_accessed=6 * dl * ffl, transcendentals=rows * ffl
         ),
-    )(tokens, cotangent, routes, gate_prob, w_gate[0], w_up[0], w_down[0])
-    total = lax.psum(tok_part, "expert")
+    )(tokens, cotangent, routes.T, gate_prob.T, w_gate[0], w_up[0], w_down[0])
+    bits = [1 << k for k in range((n_expert - 1).bit_length())]
+    mixed = expert_sum(mix_part, n_expert, bits)
+    grad_tokens = expert_sum(grad_part, n_expert, bits[::-1])
     group = next(g for g in (4, 2, 1) if chunks % g == 0)
-    grad_gate, grad_up, grad_down = pl.pallas_call(
-        grads_kernel,
+    full = pl.BlockSpec((rows, dl), lambda j: (0, 0))
+    act_block = pl.BlockSpec((group, rows, 3 * f), lambda j: (j, 0, 0))
+    wide = pl.BlockSpec((dl, group * f), lambda j: (0, j))
+    roomy = pltpu.CompilerParams(vmem_limit_bytes=60 * 1024 * 1024)
+    grad_gate, grad_up = pl.pallas_call(
+        grads_in_kernel,
         grid=(chunks // group,),
-        out_shape=(
-            jax.ShapeDtypeStruct((dl, ffl), F32),
-            jax.ShapeDtypeStruct((dl, ffl), F32),
-            jax.ShapeDtypeStruct((ffl, dl), F32),
-        ),
-        in_specs=[
-            pl.BlockSpec((group, rows, 3 * f), lambda j: (j, 0, 0)),
-            pl.BlockSpec((rows, dl), lambda j: (0, 0)),
-            pl.BlockSpec((rows, dl), lambda j: (0, 0)),
-        ],
-        out_specs=(
-            pl.BlockSpec((dl, group * f), lambda j: (0, j)),
-            pl.BlockSpec((dl, group * f), lambda j: (0, j)),
-            pl.BlockSpec((group * f, dl), lambda j: (j, 0)),
-        ),
+        out_shape=(jax.ShapeDtypeStruct((dl, ffl), F32),) * 2,
+        in_specs=[act_block, full],
+        out_specs=(wide, wide),
         scratch_shapes=[pltpu.VMEM((dl, rows), BF16)],
-        compiler_params=pltpu.CompilerParams(vmem_limit_bytes=48 * 1024 * 1024),
+        compiler_params=roomy,
         cost_estimate=pl.CostEstimate(
-            flops=6 * rows * dl * ffl, bytes_accessed=12 * dl * ffl, transcendentals=0
-        ),
-    )(act, x_all, dz_all)
-    return (total[0], total[1], grad_gate[None], grad_up[None], grad_down[None])
+            flops=4 * rows * dl * ffl, bytes_accessed=8 * dl * ffl, transcendentals=0
+        ),
+    )(act, x_all)
+    grad_down = pl.pallas_call(
+        grad_down_kernel,
+        grid=(chunks // group,),
+        out_shape=jax.ShapeDtypeStruct((ffl, dl), F32),
+        in_specs=[act_block, full],
+        out_specs=pl.BlockSpec((group * f, dl), lambda j: (j, 0)),
+        compiler_params=roomy,
+        cost_estimate=pl.CostEstimate(
+            flops=2 * rows * dl * ffl, bytes_accessed=4 * dl * ffl, transcendentals=0
+        ),
+    )(act, dz_all)
+    return (mixed, grad_tokens, grad_gate[None], grad_up[None], grad_down[None])
 
 
 def solution(mesh):
     return jax.shard_map(
-        functools.partial(per_device, mesh.shape["shard"], mesh.shape["dp"]),
+        functools.partial(per_device, mesh.shape["shard"], mesh.shape["dp"], mesh.shape["expert"]),
         mesh=mesh,
         in_specs=(
             P("dp", "shard"),

time: 201 us -> 162 us (0.81)
  waiting for transfers between devices: 21.3 us -> 0.01 us
  between operations: 14 us -> 0.68 us
  local copies, waits for them, and re-layouts: 9.02 us -> 0.01 us
  starting transfers between devices: 0.04 us -> 4.28 us
    psum x1 -> x0, waiting for transfers between devices: 21.3 us -> none  [per_device(): total = lax.psum(tok_part, 'expert')]
    pallas_call x1, Pallas kernels: 138 us -> 129 us  [per_device(): pl.pallas_call(functools.partial(exchange_kernel, n, n_dp, chunks), out_s...]
    pallas_call x1 -> x2, Pallas kernels: 18.3 us -> 25.9 us  [the longest x1 15.7 us: per_device(): pl.pallas_call(grads_in_kernel, grid=(chunks // group,), out_shape=(jax.S...]
    unnamed x8 -> x4, local copies, waits for them, and re-layouts: 7.17 us -> 0.01 us
    ppermute x0 -> x4, starting transfers between devices: none -> 4.28 us  [expert_sum(): lax.ppermute(value, 'expert', [(i, i ^ bit) for i in range(n_expert)])]
  transfers between devices with their start and end apart: 1 -> 4, of which waited for: 1 -> 0; matrix products, arithmetic and copies ran while one was open for 0% -> 1% of each run, Pallas kernels for 9% -> 16%
where the time goes in v2:
time: 162 us; the launch traced here: 161 us
  Pallas kernels  155 us (96%)
  starting transfers between devices  4.28 us (3%)
  other arithmetic  1.67 us (1%)
    pallas_call x1, Pallas kernels, per_device(): pl.pallas_call(functools.partial(exchange_kernel, n, n_dp, chunks), out_s...  129 us
    pallas_call x1, Pallas kernels, per_device(): pl.pallas_call(grads_in_kernel, grid=(chunks // group,), out_shape=(jax.S...  15.7 us
    pallas_call x1, Pallas kernels, per_device(): pl.pallas_call(grad_down_kernel, grid=(chunks // group,), out_shape=jax.S...  10.3 us
    ppermute x4, starting transfers between devices, expert_sum(): lax.ppermute(value, 'expert', [(i, i ^ bit) for i in range(n_expert)])  4.28 us
  transfers between devices with their start and end apart: 4, of which 0 were waited for; matrix products, arithmetic and copies ran while one was open for 1% of the time, Pallas kernels for 16%

profile of v2, /device:TPU:0, one launch (start us, length us, event | category | flops | bytes accessed | tf_op | source)
XLA Modules:
  0.0 161.2 jit_solution(6947808922691537419)
XLA Ops:
  0.6 128.6 %shard_map.110 = (bf16[128,1024]{1,0:T(8,128)(2,1)}, bf16[128,1024]{1,0:T(8,128)(2,1)}, bf16[32,192,384]{2,1,0:T(8,128)(2,1)}, bf16[192,1024]{1,0:T(8,128)(2,1)}, bf16[192,1024]{1,0:T(8,128)(2,1)}) custom-call(bf16[128,1024]{1,0:T(8,128)(2,1)} %tok.1, bf16[128,1024]{1,0:T(8,128)(2,1)} %cot.1, s32[2,128]{1,0:T(2,128)} %bitcast.12, f32[2,128]{1,0:T(2,128)} %bitcast.13, ...), custom_call_target="tpu_custom_call" | custom-call | flops 9663676416 | bytes 25165824 | tf_op jit(solution)/shard_map/pallas_call | solution.py:304
  129.2 0.0 copy-start.1
  129.2 0.0 copy-start
  129.2 1.6 collective-permute-start.2
  130.8 1.5 collective-permute-start
  132.3 15.7 %shard_map.111 = (f32[1024,4096]{1,0:T(8,128)}, f32[1024,4096]{1,0:T(8,128)}) custom-call(bf16[32,192,384]{2,1,0:T(8,128)(2,1)} %get-tuple-element.14.act, bf16[192,1024]{1,0:T(8,128)(2,1)} %get-tuple-element.15.x), custom_call_target="tpu_custom_call" | custom-call | flops 3221225472 | bytes 33554432 | tf_op jit(solution)/shard_map/pallas_call | solution.py:359
  148.0 0.0 collective-permute-done.2
  148.0 0.0 copy-done.1
  148.0 0.1 add_convert_fusion.1
  148.1 0.6 collective-permute-start.3
  148.7 0.0 collective-permute-done
  148.7 0.0 copy-done
  148.7 0.1 add_convert_fusion.3
  148.8 0.6 collective-permute-start.1
  149.4 10.3 %shard_map.112 = f32[4096,1024]{1,0:T(8,128)} custom-call(bf16[32,192,384]{2,1,0:T(8,128)(2,1)} %get-tuple-element.14.act, bf16[192,1024]{1,0:T(8,128)(2,1)} %get-tuple-element.18.dz), custom_call_target="tpu_custom_call" | custom-call | flops 1610612736 | bytes 16777216 | tf_op jit(solution)/shard_map/pallas_call | solution.py:371
  159.6 0.0 collective-permute-done.3
  159.6 0.8 add_convert_fusion
  160.4 0.0 collective-permute-done.1
  160.4 0.8 add_convert_fusion.2
Async XLA Ops:
  129.2 18.8 %copy-start.1 = (bf16[128,1024]{1,0:T(8,128)(2,1)S(1)}, bf16[128,1024]{1,0:T(8,128)(2,1)}, u32[]{:S(2)}) copy-start(bf16[128,1024]{1,0:T(8,128)(2,1)} %get-tuple-element.13) | copy-start | bytes 786436
  129.2 19.5 %copy-start = (bf16[128,1024]{1,0:T(8,128)(2,1)S(1)}, bf16[128,1024]{1,0:T(8,128)(2,1)}, u32[]{:S(2)}) copy-start(bf16[128,1024]{1,0:T(8,128)(2,1)} %get-tuple-element.12) | copy-start | bytes 786436
  129.2 18.8 %collective-permute-start.2 = (bf16[128,1024]{1,0:T(8,128)(2,1)}, bf16[128,1024]{1,0:T(8,128)(2,1)S(1)}, u32[]{:S(2)}, u32[]{:S(2)}) collective-permute-start(bf16[128,1024]{1,0:T(8,128)(2,1)} %get-tuple-element.13), channel_id=1, source_target_pairs={{0,8},{4,12},{8,0},{12,4},{1,9},{5,13},{9,1},{13,5},{2,10},{6,14},... | collective-permute-start | bytes 786440 | tf_op jit(solution)/shard_map/ppermute | solution.py:289
  130.8 17.9 %collective-permute-start = (bf16[128,1024]{1,0:T(8,128)(2,1)}, bf16[128,1024]{1,0:T(8,128)(2,1)S(1)}, u32[]{:S(2)}, u32[]{:S(2)}) collective-permute-start(bf16[128,1024]{1,0:T(8,128)(2,1)} %get-tuple-element.12), channel_id=1, source_target_pairs={{0,4},{4,0},{8,12},{12,8},{1,5},{5,1},{9,13},{13,9},{2,6},{6,2},{1... | collective-permute-start | bytes 786440 | tf_op jit(solution)/shard_map/ppermute | solution.py:289
  148.1 11.5 %collective-permute-start.3 = (bf16[128,1024]{1,0:T(8,128)(2,1)S(1)}, bf16[128,1024]{1,0:T(8,128)(2,1)S(1)}, u32[]{:S(2)}, u32[]{:S(2)}) collective-permute-start(bf16[128,1024]{1,0:T(8,128)(2,1)S(1)} %add_convert_fusion.1), channel_id=1, source_target_pairs={{0,4},{4,0},{8,12},{12,8},{1,5},{5,1},{9,13},{13,9},{2,6},{6,2},{1... | collective-permute-start | bytes 786440 | tf_op jit(solution)/shard_map/ppermute | solution.py:289
  148.8 11.6 %collective-permute-start.1 = (bf16[128,1024]{1,0:T(8,128)(2,1)S(1)}, bf16[128,1024]{1,0:T(8,128)(2,1)S(1)}, u32[]{:S(2)}, u32[]{:S(2)}) collective-permute-start(bf16[128,1024]{1,0:T(8,128)(2,1)S(1)} %add_convert_fusion.3), channel_id=1, source_target_pairs={{0,8},{4,12},{8,0},{12,4},{1,9},{5,13},{9,1},{13,5},{2,10},{6,14},... | collective-permute-start | bytes 786440 | tf_op jit(solution)/shard_map/ppermute | solution.py:289

commit v3 on v2

--- a/solution.py
+++ b/solution.py
@@ -11,6 +11,7 @@
 WIDTH = 128
 HOP = 3
 EARLY = 8
+HALVES = 2
 MESH = pl.DeviceIdType.MESH
 F32 = jnp.float32
 BF16 = jnp.bfloat16
@@ -32,7 +33,7 @@
     n, n_dp, chunks,
     tok, cot, routes, prob, wg, wu, wd,
     mix_out, grad_out, act_out, x_out, dz_out,
-    wgv, wuv, wdv, part, from_left, from_right, to_right, to_left,
+    wguv, wdv, part, from_left, from_right, to_right, to_left,
     x_v, dz_v, acc_o, acc_g, stage, landed, disp, wgt,
     w_sem, sr_sem, rr_sem, sl_sem, rl_sem, act_sem, xo_sem,
     xs_sem, xr_sem, os_sem, or_sem,
@@ -45,12 +46,13 @@
     n_part = part.shape[0]
     n_stage = to_right.shape[0]
     t = tok.shape[0]
+    half = part.shape[1] // HALVES
 
     def w_copies(c):
         cols = pl.ds(pl.multiple_of(c * f, f), f)
         return (
-            pltpu.make_async_copy(wg.at[:, cols], wgv.at[c], w_sem.at[0, c]),
-            pltpu.make_async_copy(wu.at[:, cols], wuv.at[c], w_sem.at[1, c]),
+            pltpu.make_async_copy(wg.at[:, cols], wguv.at[c, :, pl.ds(0, f)], w_sem.at[0, c]),
+            pltpu.make_async_copy(wu.at[:, cols], wguv.at[c, :, pl.ds(f, f)], w_sem.at[1, c]),
             pltpu.make_async_copy(wd.at[cols, :], wdv.at[c], w_sem.at[2, c]),
         )
 
@@ -120,29 +122,32 @@
     x_store.start()
     dz_store.start()
 
-    def right_copy(c):
+    def rows_of(h):
+        return pl.ds(h * half, half)
+
+    def right_copy(c, h):
         here = lax.rem(c, n_stage)
         return pltpu.make_async_remote_copy(
-            src_ref=to_right.at[here], dst_ref=from_left.at[c],
-            send_sem=sr_sem.at[here], recv_sem=rr_sem.at[c],
+            src_ref=to_right.at[here, rows_of(h)], dst_ref=from_left.at[c, rows_of(h)],
+            send_sem=sr_sem.at[here, h], recv_sem=rr_sem.at[c, h],
             device_id={"shard": lax.min(s + 1, n - 1)}, device_id_type=MESH,
         )
 
-    def left_copy(c):
+    def left_copy(c, h):
         here = lax.rem(c, n_stage)
         return pltpu.make_async_remote_copy(
-            src_ref=to_left.at[here], dst_ref=from_right.at[c],
-            send_sem=sl_sem.at[here], recv_sem=rl_sem.at[c],
+            src_ref=to_left.at[here, rows_of(h)], dst_ref=from_right.at[c, rows_of(h)],
+            send_sem=sl_sem.at[here, h], recv_sem=rl_sem.at[c, h],
             device_id={"shard": lax.max(s - 1, 0)}, device_id_type=MESH,
         )
 
-    def send(copy_of, buffer, c, value):
+    def send(copy_of, buffer, c, h, value):
         @pl.when(c >= n_stage)
         def _():
-            copy_of(c - n_stage).wait_send()
-
-        buffer[lax.rem(c, n_stage)] = value().astype(BF16)
-        copy_of(c).start()
+            copy_of(c - n_stage, h).wait_send()
+
+        buffer[lax.rem(c, n_stage), rows_of(h)] = value.astype(BF16)
+        copy_of(c, h).start()
 
     @pl.loop(0, chunks + HOP * (n - 1))
     def _(i):
@@ -157,37 +162,42 @@
                     copy.start()
 
             p = lax.rem(i, n_part)
-            part[p, :, 0:f] = dot_nn(x_v[...], wgv[i])
-            part[p, :, f:2 * f] = dot_nn(x_v[...], wuv[i])
+            part[p, :, 0:2 * f] = dot_nn(x_v[...], wguv[i])
             part[p, :, 2 * f:3 * f] = dot_nt(dz_v[...], wdv[i])
 
             @pl.when((s == 0) & (n > 1))
             def _():
-                send(right_copy, to_right, i, lambda: part[p])
+                for h in range(HALVES):
+                    send(right_copy, to_right, i, h, part[p, rows_of(h)])
 
             @pl.when((s == n - 1) & (n > 1))
             def _():
-                send(left_copy, to_left, i, lambda: part[p])
+                for h in range(HALVES):
+                    send(left_copy, to_left, i, h, part[p, rows_of(h)])
 
         r = i - HOP * s
 
         @pl.when((s > 0) & (r >= 0) & (r < chunks))
         def _():
-            right_copy(r).wait_recv()
-
-            @pl.when(s < n - 1)
-            def _():
-                send(right_copy, to_right, r, lambda: part[lax.rem(r, n_part)] + from_left[r].astype(F32))
+            for h in range(HALVES):
+                right_copy(r, h).wait_recv()
+
+                @pl.when(s < n - 1)
+                def _(h=h):
+                    own = part[lax.rem(r, n_part), rows_of(h)]
+                    send(right_copy, to_right, r, h, own + from_left[r, rows_of(h)].astype(F32))
 
         q = i - HOP * (n - 1 - s)
 
         @pl.when((s < n - 1) & (q >= 0) & (q < chunks))
         def _():
-            left_copy(q).wait_recv()
-
-            @pl.when(s > 0)
-            def _():
-                send(left_copy, to_left, q, lambda: part[lax.rem(q, n_part)] + from_right[q].astype(F32))
+            for h in range(HALVES):
+                left_copy(q, h).wait_recv()
+
+                @pl.when(s > 0)
+                def _(h=h):
+                    own = part[lax.rem(q, n_part), rows_of(h)]
+                    send(left_copy, to_left, q, h, own + from_right[q, rows_of(h)].astype(F32))
 
         c = i - HOP * lax.max(s, n - 1 - s)
 
@@ -217,7 +227,7 @@
             act[c, :, 2 * f:3 * f] = d_up
             pltpu.make_async_copy(act.at[c], act_out.at[c], act_sem.at[c]).start()
             acc_o[...] += dot_nn(hidden, wdv[c])
-            acc_g[...] += dot_nt(d_gate, wgv[c]) + dot_nt(d_up, wuv[c])
+            acc_g[...] += dot_nt(jnp.concatenate([d_gate, d_up], axis=1), wguv[c])
 
     stage[0] = acc_o[...].astype(BF16)
     stage[1] = acc_g[...].astype(BF16)
@@ -258,30 +268,30 @@
     def _(c):
         @pl.when(s < n - 1)
         def _():
-            right_copy(c).wait_send()
+            for h in range(HALVES):
+                right_copy(c, h).wait_send()
 
         @pl.when(s > 0)
         def _():
-            left_copy(c).wait_send()
-
-
-def grads_in_kernel(act, x, gate_out, up_out, x_t):
-    f = WIDTH
-
+            for h in range(HALVES):
+                left_copy(c, h).wait_send()
+
+
+def side_by_side(block):
+    return jnp.concatenate([block[c] for c in range(block.shape[0])], axis=1)
+
+
+def grads_in_kernel(d_gate, d_up, x, gate_out, up_out, x_t):
     @pl.when(pl.program_id(0) == 0)
     def _():
         x_t[...] = x[...].T
 
-    for c in range(act.shape[0]):
-        cols = slice(c * f, (c + 1) * f)
-        gate_out[:, cols] = dot_nn(x_t[...], act[c, :, f:2 * f])
-        up_out[:, cols] = dot_nn(x_t[...], act[c, :, 2 * f:3 * f])
-
-
-def grad_down_kernel(act, dz, down_out):
-    f = WIDTH
-    for c in range(act.shape[0]):
-        down_out[c * f:(c + 1) * f, :] = dot_tn(act[c, :, 0:f], dz[...])
+    gate_out[...] = dot_nn(x_t[...], side_by_side(d_gate))
+    up_out[...] = dot_nn(x_t[...], side_by_side(d_up))
+
+
+def grad_down_kernel(hidden, dz, down_out):
+    down_out[...] = dot_tn(side_by_side(hidden), dz[...])
 
 
 def expert_sum(value, n_expert, bits):
@@ -313,8 +323,7 @@
         in_specs=[vmem] * 4 + [hbm] * 3,
         out_specs=(vmem, vmem, hbm, hbm, hbm),
         scratch_shapes=[
-            pltpu.VMEM((chunks, dl, f), BF16),
-            pltpu.VMEM((chunks, dl, f), BF16),
+            pltpu.VMEM((chunks, dl, 2 * f), BF16),
             pltpu.VMEM((chunks, f, dl), BF16),
             pltpu.VMEM((n_part, rows, 3 * f), F32),
             pltpu.VMEM((chunks, rows, 3 * f), BF16),
@@ -330,10 +339,10 @@
             pltpu.VMEM((CAP, t), BF16),
             pltpu.VMEM((t, 128), F32),
             pltpu.SemaphoreType.DMA((3, chunks)),
-            pltpu.SemaphoreType.DMA((n_stage,)),
-            pltpu.SemaphoreType.DMA((chunks,)),
-            pltpu.SemaphoreType.DMA((n_stage,)),
-            pltpu.SemaphoreType.DMA((chunks,)),
+            pltpu.SemaphoreType.DMA((n_stage, HALVES)),
+            pltpu.SemaphoreType.DMA((chunks, HALVES)),
+            pltpu.SemaphoreType.DMA((n_stage, HALVES)),
+            pltpu.SemaphoreType.DMA((chunks, HALVES)),
             pltpu.SemaphoreType.DMA((chunks,)),
             pltpu.SemaphoreType.DMA((2,)),
             pltpu.SemaphoreType.DMA((2, n_dp)),
@@ -353,26 +362,28 @@
     grad_tokens = expert_sum(grad_part, n_expert, bits[::-1])
     group = next(g for g in (4, 2, 1) if chunks % g == 0)
     full = pl.BlockSpec((rows, dl), lambda j: (0, 0))
-    act_block = pl.BlockSpec((group, rows, 3 * f), lambda j: (j, 0, 0))
+    hidden_block, d_gate_block, d_up_block = (
+        pl.BlockSpec((group, rows, f), lambda j, k=k: (j, 0, k)) for k in range(3)
+    )
     wide = pl.BlockSpec((dl, group * f), lambda j: (0, j))
     roomy = pltpu.CompilerParams(vmem_limit_bytes=60 * 1024 * 1024)
     grad_gate, grad_up = pl.pallas_call(
         grads_in_kernel,
         grid=(chunks // group,),
         out_shape=(jax.ShapeDtypeStruct((dl, ffl), F32),) * 2,
-        in_specs=[act_block, full],
+        in_specs=[d_gate_block, d_up_block, full],
         out_specs=(wide, wide),
         scratch_shapes=[pltpu.VMEM((dl, rows), BF16)],
         compiler_params=roomy,
         cost_estimate=pl.CostEstimate(
             flops=4 * rows * dl * ffl, bytes_accessed=8 * dl * ffl, transcendentals=0
         ),
-    )(act, x_all)
+    )(act, act, x_all)
     grad_down = pl.pallas_call(
         grad_down_kernel,
         grid=(chunks // group,),
         out_shape=jax.ShapeDtypeStruct((ffl, dl), F32),
-        in_specs=[act_block, full],
+        in_specs=[hidden_block, full],
         out_specs=pl.BlockSpec((group * f, dl), lambda j: (j, 0)),
         compiler_params=roomy,
         cost_estimate=pl.CostEstimate(

time: 162 us -> 159 us (0.981)
  Pallas kernels: 155 us -> 152 us
    pallas_call x1, Pallas kernels: 15.7 us -> 13.4 us  [per_device(): pl.pallas_call(grads_in_kernel, grid=(chunks // group,), out_shape=(jax.S...]
  transfers between devices with their start and end apart: 4 -> 4, of which waited for: 0 -> 0; matrix products, arithmetic and copies ran while one was open for 1% -> 1% of each run, Pallas kernels for 16% -> 14%
where the time goes in v3:
time: 159 us
  Pallas kernels  152 us (96%)
  starting transfers between devices  4.26 us (3%)
  other arithmetic  1.67 us (1%)
    pallas_call x1, Pallas kernels, per_device(): pl.pallas_call(functools.partial(exchange_kernel, n, n_dp, chunks), out_s...  129 us
    pallas_call x1, Pallas kernels, per_device(): pl.pallas_call(grads_in_kernel, grid=(chunks // group,), out_shape=(jax.S...  13.4 us
    pallas_call x1, Pallas kernels, per_device(): pl.pallas_call(grad_down_kernel, grid=(chunks // group,), out_shape=jax.S...  9.48 us
    ppermute x4, starting transfers between devices, expert_sum(): lax.ppermute(value, 'expert', [(i, i ^ bit) for i in range(n_expert)])  4.26 us
  transfers between devices with their start and end apart: 4, of which 0 were waited for; matrix products, arithmetic and copies ran while one was open for 1% of the time, Pallas kernels for 14%

profile of v3, /device:TPU:0, one launch (start us, length us, event | category | flops | bytes accessed | tf_op | source)
XLA Modules:
  0.0 158.6 jit_solution(9792870394408890830)
XLA Ops:
  0.6 129.1 %shard_map.110 = (bf16[128,1024]{1,0:T(8,128)(2,1)}, bf16[128,1024]{1,0:T(8,128)(2,1)}, bf16[32,192,384]{2,1,0:T(8,128)(2,1)}, bf16[192,1024]{1,0:T(8,128)(2,1)}, bf16[192,1024]{1,0:T(8,128)(2,1)}) custom-call(bf16[128,1024]{1,0:T(8,128)(2,1)} %tok.1, bf16[128,1024]{1,0:T(8,128)(2,1)} %cot.1, s32[2,128]{1,0:T(2,128)} %bitcast.12, f32[2,128]{1,0:T(2,128)} %bitcast.13, ...), custom_call_target="tpu_custom_call" | custom-call | flops 9663676416 | bytes 25165824 | tf_op jit(solution)/shard_map/pallas_call | solution.py:314
  129.7 0.0 copy-start.1
  129.7 0.0 copy-start
  129.7 1.6 collective-permute-start.2
  131.3 1.5 collective-permute-start
  132.8 13.4 %shard_map.111 = (f32[1024,4096]{1,0:T(8,128)}, f32[1024,4096]{1,0:T(8,128)}) custom-call(bf16[32,192,384]{2,1,0:T(8,128)(2,1)} %get-tuple-element.14.d_gate.d_up.hidden, bf16[32,192,384]{2,1,0:T(8,128)(2,1)} %get-tuple-element.14.d_gate.d_up.hidden, bf16[192,1024]{1,0:T(8,128)(2,1)} %get-tuple-element.15.x), custom_call_target="tpu_custom_call" | custom-call | flops 3221225472 | bytes 33554432 | tf_op jit(solution)/shard_map/pallas_call | solution.py:370
  146.3 0.0 collective-permute-done.2
  146.3 0.0 copy-done.1
  146.3 0.1 add_convert_fusion.1
  146.3 0.6 collective-permute-start.3
  147.0 0.0 collective-permute-done
  147.0 0.0 copy-done
  147.0 0.1 add_convert_fusion.3
  147.0 0.6 collective-permute-start.1
  147.6 9.5 %shard_map.112 = f32[4096,1024]{1,0:T(8,128)} custom-call(bf16[32,192,384]{2,1,0:T(8,128)(2,1)} %get-tuple-element.14.d_gate.d_up.hidden, bf16[192,1024]{1,0:T(8,128)(2,1)} %get-tuple-element.18.dz), custom_call_target="tpu_custom_call" | custom-call | flops 1610612736 | bytes 16777216 | tf_op jit(solution)/shard_map/pallas_call | solution.py:382
  157.1 0.0 collective-permute-done.3
  157.1 0.8 add_convert_fusion
  157.9 0.0 collective-permute-done.1
  157.9 0.8 add_convert_fusion.2
Async XLA Ops:
  129.7 16.5 %copy-start.1 = (bf16[128,1024]{1,0:T(8,128)(2,1)S(1)}, bf16[128,1024]{1,0:T(8,128)(2,1)}, u32[]{:S(2)}) copy-start(bf16[128,1024]{1,0:T(8,128)(2,1)} %get-tuple-element.13) | copy-start | bytes 786436
  129.7 17.2 %copy-start = (bf16[128,1024]{1,0:T(8,128)(2,1)S(1)}, bf16[128,1024]{1,0:T(8,128)(2,1)}, u32[]{:S(2)}) copy-start(bf16[128,1024]{1,0:T(8,128)(2,1)} %get-tuple-element.12) | copy-start | bytes 786436
  129.7 16.5 %collective-permute-start.2 = (bf16[128,1024]{1,0:T(8,128)(2,1)}, bf16[128,1024]{1,0:T(8,128)(2,1)S(1)}, u32[]{:S(2)}, u32[]{:S(2)}) collective-permute-start(bf16[128,1024]{1,0:T(8,128)(2,1)} %get-tuple-element.13), channel_id=1, source_target_pairs={{0,8},{4,12},{8,0},{12,4},{1,9},{5,13},{9,1},{13,5},{2,10},{6,14},... | collective-permute-start | bytes 786440 | tf_op jit(solution)/shard_map/ppermute | solution.py:299
  131.3 15.6 %collective-permute-start = (bf16[128,1024]{1,0:T(8,128)(2,1)}, bf16[128,1024]{1,0:T(8,128)(2,1)S(1)}, u32[]{:S(2)}, u32[]{:S(2)}) collective-permute-start(bf16[128,1024]{1,0:T(8,128)(2,1)} %get-tuple-element.12), channel_id=1, source_target_pairs={{0,4},{4,0},{8,12},{12,8},{1,5},{5,1},{9,13},{13,9},{2,6},{6,2},{1... | collective-permute-start | bytes 786440 | tf_op jit(solution)/shard_map/ppermute | solution.py:299
  146.3 10.7 %collective-permute-start.3 = (bf16[128,1024]{1,0:T(8,128)(2,1)S(1)}, bf16[128,1024]{1,0:T(8,128)(2,1)S(1)}, u32[]{:S(2)}, u32[]{:S(2)}) collective-permute-start(bf16[128,1024]{1,0:T(8,128)(2,1)S(1)} %add_convert_fusion.1), channel_id=1, source_target_pairs={{0,4},{4,0},{8,12},{12,8},{1,5},{5,1},{9,13},{13,9},{2,6},{6,2},{1... | collective-permute-start | bytes 786440 | tf_op jit(solution)/shard_map/ppermute | solution.py:299
  147.0 10.8 %collective-permute-start.1 = (bf16[128,1024]{1,0:T(8,128)(2,1)S(1)}, bf16[128,1024]{1,0:T(8,128)(2,1)S(1)}, u32[]{:S(2)}, u32[]{:S(2)}) collective-permute-start(bf16[128,1024]{1,0:T(8,128)(2,1)S(1)} %add_convert_fusion.3), channel_id=1, source_target_pairs={{0,8},{4,12},{8,0},{12,4},{1,9},{5,13},{9,1},{13,5},{2,10},{6,14},... | collective-permute-start | bytes 786440 | tf_op jit(solution)/shard_map/ppermute | solution.py:299

commit v4 on v3

--- a/solution.py
+++ b/solution.py
@@ -9,7 +9,7 @@
 
 CAP = 96
 WIDTH = 128
-HOP = 3
+HOP = 4
 EARLY = 8
 HALVES = 2
 MESH = pl.DeviceIdType.MESH
@@ -308,7 +308,7 @@
     chunks = ffl // f
     rows = n_dp * CAP
     n_part = min(HOP * (n - 1) + 1, chunks)
-    n_stage = max(1, min(4, chunks // 2))
+    n_stage = max(1, min(8, chunks // 2))
     vmem = pl.BlockSpec(memory_space=pltpu.VMEM)
     hbm = pl.BlockSpec(memory_space=pl.ANY)
     mix_part, grad_part, act, x_all, dz_all = pl.pallas_call(

time: 159 us -> 162 us (1.019)
  Pallas kernels: 152 us -> 155 us
    pallas_call x1, Pallas kernels: 129 us -> 132 us  [per_device(): pl.pallas_call(functools.partial(exchange_kernel, n, n_dp, chunks), out_s...]
where the time goes in v4:
time: 162 us
  Pallas kernels  155 us (96%)
  starting transfers between devices  4.27 us (3%)
  other arithmetic  1.67 us (1%)
    pallas_call x1, Pallas kernels, per_device(): pl.pallas_call(functools.partial(exchange_kernel, n, n_dp, chunks), out_s...  132 us
    pallas_call x1, Pallas kernels, per_device(): pl.pallas_call(grads_in_kernel, grid=(chunks // group,), out_shape=(jax.S...  13.4 us
    pallas_call x1, Pallas kernels, per_device(): pl.pallas_call(grad_down_kernel, grid=(chunks // group,), out_shape=jax.S...  9.47 us
    ppermute x4, starting transfers between devices, expert_sum(): lax.ppermute(value, 'expert', [(i, i ^ bit) for i in range(n_expert)])  4.27 us
  transfers between devices with their start and end apart: 4, of which 0 were waited for; matrix products, arithmetic and copies ran while one was open for 1% of the time, Pallas kernels for 14%

profile of v4, /device:TPU:0, one launch (start us, length us, event | category | flops | bytes accessed | tf_op | source)
XLA Modules:
  0.0 162.0 jit_solution(9652628823231512331)
XLA Ops:
  0.6 132.4 %shard_map.110 = (bf16[128,1024]{1,0:T(8,128)(2,1)}, bf16[128,1024]{1,0:T(8,128)(2,1)}, bf16[32,192,384]{2,1,0:T(8,128)(2,1)}, bf16[192,1024]{1,0:T(8,128)(2,1)}, bf16[192,1024]{1,0:T(8,128)(2,1)}) custom-call(bf16[128,1024]{1,0:T(8,128)(2,1)} %tok.1, bf16[128,1024]{1,0:T(8,128)(2,1)} %cot.1, s32[2,128]{1,0:T(2,128)} %bitcast.12, f32[2,128]{1,0:T(2,128)} %bitcast.13, ...), custom_call_target="tpu_custom_call" | custom-call | flops 9663676416 | bytes 25165824 | tf_op jit(solution)/shard_map/pallas_call | solution.py:314
  133.1 0.0 copy-start.1
  133.1 0.0 copy-start
  133.1 1.6 collective-permute-start.2
  134.7 1.5 collective-permute-start
  136.2 13.4 %shard_map.111 = (f32[1024,4096]{1,0:T(8,128)}, f32[1024,4096]{1,0:T(8,128)}) custom-call(bf16[32,192,384]{2,1,0:T(8,128)(2,1)} %get-tuple-element.14.d_gate.d_up.hidden, bf16[32,192,384]{2,1,0:T(8,128)(2,1)} %get-tuple-element.14.d_gate.d_up.hidden, bf16[192,1024]{1,0:T(8,128)(2,1)} %get-tuple-element.15.x), custom_call_target="tpu_custom_call" | custom-call | flops 3221225472 | bytes 33554432 | tf_op jit(solution)/shard_map/pallas_call | solution.py:370
  149.6 0.0 collective-permute-done.2
  149.6 0.0 copy-done.1
  149.6 0.1 add_convert_fusion.1
  149.7 0.6 collective-permute-start.3
  150.3 0.0 collective-permute-done
  150.3 0.0 copy-done
  150.3 0.1 add_convert_fusion.3
  150.4 0.6 collective-permute-start.1
  151.0 9.5 %shard_map.112 = f32[4096,1024]{1,0:T(8,128)} custom-call(bf16[32,192,384]{2,1,0:T(8,128)(2,1)} %get-tuple-element.14.d_gate.d_up.hidden, bf16[192,1024]{1,0:T(8,128)(2,1)} %get-tuple-element.18.dz), custom_call_target="tpu_custom_call" | custom-call | flops 1610612736 | bytes 16777216 | tf_op jit(solution)/shard_map/pallas_call | solution.py:382
  160.4 0.0 collective-permute-done.3
  160.4 0.8 add_convert_fusion
  161.2 0.0 collective-permute-done.1
  161.2 0.8 add_convert_fusion.2
Async XLA Ops:
  133.1 16.6 %copy-start.1 = (bf16[128,1024]{1,0:T(8,128)(2,1)S(1)}, bf16[128,1024]{1,0:T(8,128)(2,1)}, u32[]{:S(2)}) copy-start(bf16[128,1024]{1,0:T(8,128)(2,1)} %get-tuple-element.13) | copy-start | bytes 786436
  133.1 17.2 %copy-start = (bf16[128,1024]{1,0:T(8,128)(2,1)S(1)}, bf16[128,1024]{1,0:T(8,128)(2,1)}, u32[]{:S(2)}) copy-start(bf16[128,1024]{1,0:T(8,128)(2,1)} %get-tuple-element.12) | copy-start | bytes 786436
  133.1 16.5 %collective-permute-start.2 = (bf16[128,1024]{1,0:T(8,128)(2,1)}, bf16[128,1024]{1,0:T(8,128)(2,1)S(1)}, u32[]{:S(2)}, u32[]{:S(2)}) collective-permute-start(bf16[128,1024]{1,0:T(8,128)(2,1)} %get-tuple-element.13), channel_id=1, source_target_pairs={{0,8},{4,12},{8,0},{12,4},{1,9},{5,13},{9,1},{13,5},{2,10},{6,14},... | collective-permute-start | bytes 786440 | tf_op jit(solution)/shard_map/ppermute | solution.py:299
  134.7 15.6 %collective-permute-start = (bf16[128,1024]{1,0:T(8,128)(2,1)}, bf16[128,1024]{1,0:T(8,128)(2,1)S(1)}, u32[]{:S(2)}, u32[]{:S(2)}) collective-permute-start(bf16[128,1024]{1,0:T(8,128)(2,1)} %get-tuple-element.12), channel_id=1, source_target_pairs={{0,4},{4,0},{8,12},{12,8},{1,5},{5,1},{9,13},{13,9},{2,6},{6,2},{1... | collective-permute-start | bytes 786440 | tf_op jit(solution)/shard_map/ppermute | solution.py:299
  149.7 10.7 %collective-permute-start.3 = (bf16[128,1024]{1,0:T(8,128)(2,1)S(1)}, bf16[128,1024]{1,0:T(8,128)(2,1)S(1)}, u32[]{:S(2)}, u32[]{:S(2)}) collective-permute-start(bf16[128,1024]{1,0:T(8,128)(2,1)S(1)} %add_convert_fusion.1), channel_id=1, source_target_pairs={{0,4},{4,0},{8,12},{12,8},{1,5},{5,1},{9,13},{13,9},{2,6},{6,2},{1... | collective-permute-start | bytes 786440 | tf_op jit(solution)/shard_map/ppermute | solution.py:299
  150.4 10.8 %collective-permute-start.1 = (bf16[128,1024]{1,0:T(8,128)(2,1)S(1)}, bf16[128,1024]{1,0:T(8,128)(2,1)S(1)}, u32[]{:S(2)}, u32[]{:S(2)}) collective-permute-start(bf16[128,1024]{1,0:T(8,128)(2,1)S(1)} %add_convert_fusion.3), channel_id=1, source_target_pairs={{0,8},{4,12},{8,0},{12,4},{1,9},{5,13},{9,1},{13,5},{2,10},{6,14},... | collective-permute-start | bytes 786440 | tf_op jit(solution)/shard_map/ppermute | solution.py:299
